TPU v7x, 32 devices: a whole 2x2x4 slice. The times are simulated.
32 devices in a mesh: leaf: 2 (over y), row: 2 (over x), col: 8 (over z, core).
Axes of the slice: x: 2, y: 2, z: 4, core: 2. Of those that a mesh axis runs over, the one named last changes fastest.
Arguments:
- front_window: float32 [49152, 2048], P(('leaf', 'row'), 'col'), parts along dimension 0, may hold values from -8 to 785
- children: float32 [65536, 2048], P(('leaf', 'row', 'col')), parts along dimension 0, may hold values from -1 to 1
- row_map: int32 [4, 128], P('leaf'), parts along dimension 0, may hold values from 0 to 191, as said below
- col_map: int32 [4, 16], P('leaf'), parts along dimension 0, may hold values from 0 to 15, as said below
Outputs:
- factored: float32 [49152, 2048], P(('leaf', 'row'), 'col'), parts along dimension 0
There are 2 independent parts, one for each index of `leaf`. A program takes and returns all parts, laid end to end along the dimension named above; each array names one. Nothing has to cross between parts.
Inputs may be any that keep to these rules, and one draw needn't show every extreme that they name: `row_map`: for each sibling, its entries are distinct; each aligned run of 128 of its row blocks names exactly 64 blocks in each range of 96 consecutive parent blocks. `col_map`: each sibling's row is a permutation of the 16 window blocks.
All inputs are finite; a program needn't handle non-finite values.
Results may differ from a plain program's by a relative error of at most 0.000088.
Values sent between devices are 32-bit elements; how exact they have to be, the bound alone decides.
A program may use at most 192 MiB of HBM per device.

v0:
```python
import jax
import jax.numpy as jnp
from jax import lax
from jax.sharding import PartitionSpec as P

BLK = 128
PANEL = 256


def broadcast(value, axis, source):
    kept = jnp.where(lax.axis_index(axis) == source, value, 0).astype(value.dtype)
    return lax.psum(kept, axis)


def body(front_window, children, row_map, col_map):
    row_count = lax.axis_size("row")
    col_count = lax.axis_size("col")
    row_index = lax.axis_index("row")
    col_index = lax.axis_index("col")
    rows_here, cols_here = front_window.shape
    child_rows = children.shape[0]
    window_blocks = children.shape[1] // BLK
    sibling = row_index // (row_count // 2)
    chosen_cols = lax.dynamic_index_in_dim(col_map, sibling, 0, keepdims=False)
    inverse_cols = jnp.argsort(chosen_cols)
    spread = jnp.take(children.reshape(child_rows, window_blocks, BLK), inverse_cols, axis=1)
    spread = spread.reshape(child_rows, col_count, cols_here)
    quarter = lax.all_to_all(spread, "col", split_axis=1, concat_axis=0, tiled=True)
    quarter = quarter.reshape(col_count * child_rows, cols_here)
    quarter_blocks = quarter.shape[0] // BLK
    capacity = quarter_blocks // row_count
    parent_blocks = rows_here // BLK
    source_maps = row_map.reshape(row_count, quarter_blocks)
    owners = source_maps // parent_blocks
    ordering = jnp.argsort(owners, axis=1, stable=True)
    own_order = lax.dynamic_index_in_dim(ordering, row_index, 0, keepdims=False)
    outgoing = jnp.take(quarter.reshape(quarter_blocks, BLK, cols_here), own_order, axis=0)
    outgoing = outgoing.reshape(row_count, capacity * BLK, cols_here)
    incoming = lax.all_to_all(outgoing, "row", split_axis=0, concat_axis=0, tiled=True)
    chosen = lax.dynamic_slice_in_dim(ordering, row_index * capacity, capacity, axis=1)
    targets = (jnp.take_along_axis(source_maps, chosen, axis=1) % parent_blocks).reshape(-1)
    selector = (targets[:, None] == jnp.arange(parent_blocks, dtype=jnp.int32)[None, :]).astype(
        jnp.float32
    )
    added = jnp.einsum(
        "sp,sk->pk",
        selector,
        incoming.reshape(row_count * capacity, BLK * cols_here),
        precision=lax.Precision.HIGHEST,
    )
    assembled = front_window + added.reshape(rows_here, cols_here)
    identity = jnp.eye(PANEL, dtype=jnp.float32)
    global_rows = row_index * rows_here + jnp.arange(rows_here, dtype=jnp.int32)
    panel_rows = broadcast(assembled, "col", 0)
    diagonal_block = broadcast(panel_rows[:PANEL], "row", 0)
    factor = jnp.linalg.cholesky(diagonal_block)
    inverse = jax.scipy.linalg.solve_triangular(factor, identity, lower=True)
    solved = jnp.dot(panel_rows, inverse.T, precision=lax.Precision.HIGHEST)
    leading = jnp.where(row_index == 0, factor, solved[:PANEL])
    lower_panel = jnp.concatenate([leading, solved[PANEL:]], axis=0)
    owner_row = col_index * cols_here // rows_here
    start = jnp.clip(col_index * cols_here - row_index * rows_here, 0, rows_here - cols_here)
    piece = lax.dynamic_slice_in_dim(lower_panel, start, cols_here, 0)
    matching = broadcast(piece, "row", owner_row)
    update = jnp.dot(lower_panel, matching.T, precision=lax.Precision.HIGHEST)
    global_cols = col_index * cols_here + jnp.arange(cols_here, dtype=jnp.int32)
    inside = (global_rows >= PANEL)[:, None] & (global_cols >= PANEL)[None, :]
    result = jnp.where(inside, assembled - update, assembled)
    return jnp.where((global_cols < PANEL)[None, :], lower_panel, result)


def solution(mesh):
    placed = (
        P(("leaf", "row"), "col"),
        P(("leaf", "row", "col"), None),
        P("leaf", None),
        P("leaf", None),
    )
    return jax.shard_map(
        body, mesh=mesh, in_specs=placed, out_specs=P(("leaf", "row"), "col"), check_vma=False
    )
```

profile of v0, /device:TPU:25, one launch (start us, length us, event | category | flops | bytes accessed | tf_op | source)
XLA Modules:
  0.0 1207.5 jit_solution(6401520857214902791)
XLA Ops:
  6.5 0.7 copy-done
  7.2 1.2 sort.35
  8.5 17.6 %copy.29 = f32[2048,2048]{0,1:T(8,128)} copy(f32[2048,2048]{1,0:T(8,128)} %param.5) | data formatting | bytes 33554432 | tf_op args[1]
  26.1 17.6 %copy.30 = f32[2048,16,128]{2,0,1:T(8,128)} copy(f32[2048,16,128]{0,2,1:T(8,128)} %bitcast.65) | data formatting | bytes 33554432 | tf_op jit(solution)/shard_map/reshape | solution.py:26
  43.7 13.8 %gather_fusion = f32[16,2048,128]{2,1,0:T(8,128)} fusion(f32[2048,16,128]{2,0,1:T(8,128)} %copy.30, s32[1024]{0:T(1024)S(1)} %pad_clamp_fusion.1), kind=kCustom, calls=%fused_computation | custom fusion | bytes 33554496 | tf_op jit(solution)/shard_map/jit(_take)/gather | solution.py:26
  57.5 17.6 %copy.31 = f32[2048,16,128]{0,2,1:T(8,128)} copy(f32[2048,16,128]{2,0,1:T(8,128)} %bitcast.63) | data formatting | bytes 33554432 | tf_op jit(solution)/shard_map/jit(_take)/gather | solution.py:26
  75.4 11.4 bitcast_select_fusion.1
  86.8 5.8 all-to-all-start
  92.7 0.6 and_select_fusion.2
  93.2 0.6 iota.96
  93.9 4.2 sort.37.cloned.1.call-done
  98.0 0.7 fusion.24
  98.9 0.7 fusion.23
  99.6 353.8 %all-to-all-done = f32[2048,8,256]{0,2,1:T(8,128)} async-done(((f32[2048,8,256]{0,2,1:T(8,128)}), f32[2048,8,256]{0,2,1:T(8,128)}, u32[]{:S(2)}, u32[]{:S(2)}) %all-to-all-start) | async-done | bytes 16777248 | tf_op jit(solution)/shard_map/all_to_all | solution.py:28
  453.4 16.4 %copy.32 = f32[8,2048,1,256]{3,1,0,2:T(8,128)} copy(f32[8,2048,1,256]{1,3,0,2:T(8,128)} %bitcast.7) | data formatting | bytes 33554432 | tf_op jit(solution)/shard_map/all_to_all | solution.py:28
  469.8 15.6 %gather_fusion.1 = f32[128,128,256]{2,1,0:T(8,128)} fusion(f32[128,128,256]{2,1,0:T(8,128)} %bitcast.64, s32[1024]{0:T(1024)S(1)} %pad_clamp_fusion), kind=kCustom, calls=%fused_computation.1 | custom fusion | bytes 33554944 | tf_op jit(solution)/shard_map/jit(_take)/gather | solution.py:37
  485.5 12.2 %bitcast_select_fusion = f32[2,8192,256]{2,1,0:T(8,128)} fusion(pred[2,8192]{1,0:T(4,128)(4,1)S(1)} %bitcast.66, f32[2,8192,256]{2,1,0:T(8,128)} %bitcast.61), kind=kLoop, calls=%fused_computation.8 | loop fusion | flops 4194304 | bytes 33570816 | tf_op jit(solution)/shard_map/jit(_take)/select_n | solution.py:37
  497.6 9.7 all-to-all-start.1
  507.9 12.6 %copy.33 = f32[12288,256]{0,1:T(8,128)} copy(f32[12288,256]{1,0:T(8,128)} %param.4) | data formatting | bytes 25165824 | tf_op args[0]
  520.7 1.5 gather_fusion.2
  522.5 167.6 %all-to-all-done.1 = f32[2,8192,256]{2,1,0:T(8,128)} async-done(((f32[2,8192,256]{2,1,0:T(8,128)}), f32[2,8192,256]{2,1,0:T(8,128)}, u32[]{:S(2)}, u32[]{:S(2)}) %all-to-all-start.1) | async-done | bytes 16777248 | tf_op jit(solution)/shard_map/all_to_all | solution.py:39
  690.1 18.2 %reshape.123 = f32[128,32768]{1,0:T(8,128)} reshape(f32[2,8192,256]{2,1,0:T(8,128)} %all-to-all-done.1) | data formatting | bytes 33554432 | tf_op jit(solution)/shard_map/reshape | solution.py:48
  708.3 14.2 %fusion.17 = f32[96,32768]{1,0:T(8,128)} fusion(f32[128,32768]{1,0:T(8,128)} %reshape.123, s32[128]{0:T(128)S(1)} %and_select_fusion), kind=kOutput, calls=%fused_computation.46 | convolution fusion | flops 4831850496 | bytes 29360640 | tf_op jit(solution)/shard_map/sp,sk->pk/dot_general | solution.py:45
  722.5 13.6 %reshape.124 = f32[12288,256]{1,0:T(8,128)} reshape(f32[96,32768]{1,0:T(8,128)} %fusion.17) | data formatting | bytes 25165824 | tf_op jit(solution)/shard_map/reshape | solution.py:51
  736.1 12.6 %copy.34 = f32[12288,256]{0,1:T(8,128)} copy(f32[12288,256]{1,0:T(8,128)} %reshape.124) | data formatting | bytes 25165824 | tf_op jit(solution)/shard_map/reshape | solution.py:51
  748.7 18.5 %broadcast_select_fusion = (f32[12288,256]{0,1:T(8,128)}, f32[12288,256]{0,1:T(8,128)}) fusion(pred[]{:T(512)S(6)} %eq.31, f32[12288,256]{0,1:T(8,128)} %copy.33, f32[12288,256]{0,1:T(8,128)} %copy.34), kind=kLoop, calls=%fused_computation.13 | loop fusion | flops 6291456 | bytes 50331648 | tf_op jit(solution)/shard_map/jit(_where)/select_n | solution.py:11
  767.3 254.8 %all-reduce.5.cloned.1.call-done = f32[12288,256]{0,1:T(8,128)} async-done(((f32[12288,256]{0,1:T(8,128)}), f32[12288,256]{0,1:T(8,128)}) %all-reduce.5.cloned.1.call-update) | async-done | bytes 12582928 | tf_op jit(solution)/shard_map/psum | solution.py:12
  1022.1 1.7 slice_select_fusion.1
  1024.1 23.8 %all-reduce.7.cloned.1.call-done = f32[256,256]{0,1:T(8,128)} async-done(((f32[256,256]{0,1:T(8,128)}), f32[256,256]{0,1:T(8,128)}) %all-reduce.7.cloned.1.call-update) | async-done | bytes 262160 | tf_op jit(solution)/shard_map/psum | solution.py:12
  1048.0 1.1 copy.35
  1049.1 1.0 fusion.7
  1050.1 11.7 cholesky.49
  1061.8 9.8 custom-call.15
  1072.1 11.7 cholesky.103
  1084.2 0.7 compare_reduce_fusion
  1086.3 4.3 while.1
  1086.5 0.6 fusion.36
  1087.1 1.3 dynamic-slice.7
  1088.6 0.6 fusion.36
  1089.2 1.3 dynamic-slice.7
  1090.6 19.7 %custom-call.16 = f32[2,128,128]{1,2,0:T(8,128)S(1)} custom-call(f32[2,128,128]{2,1,0:T(8,128)S(1)} %get-tuple-element.16), custom_call_target="InvertDiagBlocksLowerTriangular" | custom-call | tf_op jit(solution)/shard_map/jit(_solve_triangular)/triangular_solve | solution.py:57
  1111.2 14.1 %fusion.3 = f32[12288,256]{0,1:T(8,128)S(1)} fusion(f32[12288,256]{0,1:T(8,128)} %all-reduce.5.cloned.1.call-done, f32[128,256]{1,0:T(8,128)S(1)} %fusion.13, f32[128,256]{1,0:T(8,128)S(1)} %fusion.10), kind=kOutput, calls=%fused_computation.19 | convolution fusion | flops 9663741952 | bytes 25427968 | tf_op jit(solution)/shard_map/dot_general | solution.py:58
  1125.3 4.8 copy-done.3
  1130.1 9.7 slice.79
  1139.8 1.9 fusion.9
  1141.8 23.3 %all-reduce.9.cloned.1.call-done = f32[256,256]{0,1:T(8,128)} async-done(((f32[256,256]{0,1:T(8,128)}), f32[256,256]{0,1:T(8,128)}) %all-reduce.9.cloned.1.call-update) | async-done | bytes 262160 | tf_op jit(solution)/shard_map/psum | solution.py:12
  1165.1 23.0 %fusion = f32[12288,256]{0,1:T(8,128)} fusion(f32[12288,256]{0,1:T(8,128)} %get-tuple-element.38, f32[256,256]{0,1:T(8,128)} %all-reduce.9.cloned.1.call-done, f32[256,256]{0,1:T(8,128)S(1)} %slice_select_fusion, f32[12032,256]{0,1:T(8,128)} %slice.79, pred[256]{0:T(512)(128)(4,1)S(1)} %get-tuple-element.44, pred[12288]{0:T(1024)(128)(4,1)S(1)} %add_compare_fusion, ...), kind=kOutput, calls=%fused_computation.10 | convolution fusion | flops 9682550784 | bytes 38023680 | tf_op jit(solution)/shard_map/dot_general | solution.py:65
  1188.1 12.6 %copy.43 = f32[12288,256]{1,0:T(8,128)} copy(f32[12288,256]{0,1:T(8,128)} %fusion) | data formatting | bytes 25165824 | tf_op jit(solution)/shard_map/jit(_where)/select_n | solution.py:69
  (63 shorter events, 4.0 us)
Async XLA Ops:
  6.5 0.7 copy-start
  86.8 5.9 copy-start.2
  86.8 366.6 %all-to-all-start = ((f32[2048,8,256]{0,2,1:T(8,128)}), f32[2048,8,256]{0,2,1:T(8,128)}, u32[]{:S(2)}, u32[]{:S(2)}) async-start(f32[2048,8,256]{0,2,1:T(8,128)} %bitcast_select_fusion.1), calls=%async_computation | async-start | bytes 33554432 | tf_op jit(solution)/shard_map/all_to_all | solution.py:28
  92.6 5.4 sort.37.cloned.1.call-start
  497.6 192.4 %all-to-all-start.1 = ((f32[2,8192,256]{2,1,0:T(8,128)}), f32[2,8192,256]{2,1,0:T(8,128)}, u32[]{:S(2)}, u32[]{:S(2)}) async-start(f32[2,8192,256]{2,1,0:T(8,128)} %bitcast_select_fusion), calls=%async_computation.1 | async-start | bytes 33554432 | tf_op jit(solution)/shard_map/all_to_all | solution.py:39
  507.3 514.8 %all-reduce.5.cloned.1.call-start = ((), (), s32[]{:S(2)}) async-start(), calls=%async_computation.2 | async-start | bytes 25165824 | tf_op jit(solution)/shard_map/psum | solution.py:12
  507.9 12.6 %copy-start.4 = (s32[2,128]{1,0:T(2,128)S(1)}, s32[2,128]{1,0:T(2,128)}, u32[]{:S(2)}) copy-start(s32[2,128]{1,0:T(2,128)} %get-tuple-element.7) | copy-start | bytes 3076
  767.3 280.7 %all-reduce.7.cloned.1.call-start = ((), (), s32[]{:S(2)}) async-start(), calls=%async_computation.3 | async-start | bytes 524288 | tf_op jit(solution)/shard_map/psum | solution.py:12
  1023.8 141.3 %all-reduce.9.cloned.1.call-start = ((), (), s32[]{:S(2)}) async-start(), calls=%async_computation.4 | async-start | bytes 524288 | tf_op jit(solution)/shard_map/psum | solution.py:12
  1125.3 4.8 copy-start.3
  1165.1 35.6 %copy-start.1 = (s32[2,16]{1,0:T(2,128)S(1)}, s32[2,16]{1,0:T(2,128)}, u32[]{:S(2)}) copy-start(s32[2,16]{1,0:T(2,128)} %param.7) | copy-start | bytes 388
Sparse Core Ops, SparseCore 0:
  95.7 2.0 sort.39.cloned.1.call-done
  767.4 254.6 all-reduce.4
  1024.5 23.4 all-reduce.6
  1141.9 23.1 all-reduce.8
  (1 shorter events, 0.0 us)
where the time goes:
time: 1220 us; the launch traced here: 1210 us
  waiting for transfers between devices  823 us (67%)
  local copies, waits for them, and re-layouts  197 us (16%)
  other arithmetic  103 us (8%)
  matrix products  52.7 us (4%)
  starting transfers between devices  16.3 us (1%)
  between operations  15 us (1%)
    all_to_all x1, waiting for transfers between devices, body(): lax.all_to_all(spread, 'col', split_axis=1, concat_axis=0, tiled=True)  354 us
    psum x3, waiting for transfers between devices, broadcast(): return lax.psum(kept, axis)  302 us
    all_to_all x1, waiting for transfers between devices, body(): lax.all_to_all(outgoing, 'row', split_axis=0, concat_axis=0, tiled=True)  168 us
    unnamed x15, local copies, waits for them, and re-layouts  35.8 us
    another operation x6, other arithmetic, body(): factor = jnp.linalg.cholesky(diagonal_block)  34 us
    gather x2, local copies, waits for them, and re-layouts, body(): jnp.take(children.reshape(child_rows, window_blocks, BLK), inverse_cols,...  31.4 us
    reshape x2, local copies, waits for them, and re-layouts, body(): assembled = front_window + added.reshape(rows_here, cols_here)  26.2 us
  transfers between devices with their start and end apart: 5, of which 5 were waited for; matrix products, arithmetic and copies ran while one was open for 1% of the time, Pallas kernels for 0%

commit v1 on v0

v1 whole, which is shorter than its diff:
```python
import functools

import jax
import jax.numpy as jnp
from jax import lax
from jax.experimental import pallas as pl
from jax.experimental.pallas import tpu as pltpu
from jax.sharding import PartitionSpec as P

BLK = 128
PANEL = 256
PB = PANEL // BLK
NCH = 8
SUB = BLK // NCH
HI = lax.Precision.HIGHEST
MESH = pl.DeviceIdType.MESH
VMEM_LIMIT = 60 * 1024 * 1024


def pack_kernel(index_ref, child_ref, out_ref):
    out_ref[0] = child_ref[...]


def pack(children, inverse_cols, col_count, cols_here):
    child_rows, width = children.shape
    per = cols_here // BLK
    return pl.pallas_call(
        pack_kernel,
        grid_spec=pltpu.PrefetchScalarGridSpec(
            num_scalar_prefetch=1,
            grid=(width // BLK,),
            in_specs=[pl.BlockSpec((child_rows, BLK), lambda k, idx: (0, idx[k]))],
            out_specs=pl.BlockSpec((1, child_rows, BLK), lambda k, idx: (k // per, 0, k % per)),
        ),
        out_shape=jax.ShapeDtypeStruct((col_count, child_rows, cols_here), jnp.float32),
        compiler_params=pltpu.CompilerParams(vmem_limit_bytes=32 * 1024 * 1024),
    )(inverse_cols, children)


def move_kernel(dims, order_ref, place_ref, send_ref, front_ref, asm_ref, panel_ref, match_ref, diag_ref, *scratch):
    C, R, nb, cap, pb = dims
    zin, xout, xin, buf = (scratch[i * NCH:(i + 1) * NCH] for i in range(4))
    zs, zr, zl, xs, xr, fl, ol, ps, pr, pl_sem, ms, mr, ml = scratch[4 * NCH:]
    c = lax.axis_index("col")
    r = lax.axis_index("row")
    even = lax.rem(c, 2) == 0

    def rows(j):
        return pl.ds(j * SUB, SUB)

    def front_copy(j):
        return pltpu.make_async_copy(front_ref.at[:, rows(j), :], buf[j], fl.at[j])

    def own_copy(j):
        return pltpu.make_async_copy(
            send_ref.at[c, :, rows(j), :], zin[j].at[pl.ds(c * nb, nb)], zl.at[j]
        )

    def z_copy(j, dest, source):
        return pltpu.make_async_remote_copy(
            src_ref=send_ref.at[dest, :, rows(j), :],
            dst_ref=zin[j].at[pl.ds(source * nb, nb)],
            send_sem=zs.at[j, dest],
            recv_sem=zr.at[j, source],
            device_id={"col": dest},
            device_id_type=MESH,
        )

    def x_copy(j, o, dest, source):
        return pltpu.make_async_remote_copy(
            src_ref=xout[j].at[o - 1],
            dst_ref=xin[j].at[pl.ds(source * cap, cap)],
            send_sem=xs.at[j, o - 1],
            recv_sem=xr.at[j, source],
            device_id={"row": dest},
            device_id_type=MESH,
        )

    def p_copy(j, source, hop):
        return pltpu.make_async_remote_copy(
            src_ref=source,
            dst_ref=panel_ref.at[:, rows(j), :],
            send_sem=ps.at[j, hop - 1],
            recv_sem=pr.at[j],
            device_id={"col": lax.rem(c + hop, C)},
            device_id_type=MESH,
        )

    def out_copy(j):
        return pltpu.make_async_copy(buf[j], asm_ref.at[:, rows(j), :], ol.at[j])

    def panel_keep(j):
        return pltpu.make_async_copy(buf[j], panel_ref.at[:, rows(j), :], pl_sem.at[j])

    for j in range(NCH):
        own_copy(j).start()
        front_copy(j).start()
        xin[j][R * cap] = jnp.zeros(xin[j].shape[1:], jnp.float32)

    barrier = pltpu.get_barrier_semaphore()
    for d in range(1, C):
        pl.semaphore_signal(barrier, inc=1, device_id={"col": lax.rem(c + d, C)}, device_id_type=MESH)
    for o in range(1, R):
        pl.semaphore_signal(barrier, inc=1, device_id={"row": lax.rem(r + o, R)}, device_id_type=MESH)
    pl.semaphore_wait(barrier, C + R - 2)

    @pl.when(c != 0)
    def _():
        for j in range(NCH):
            z_copy(j, 0, c).start()

    for j in range(NCH):

        @pl.loop(1, C)
        def _(d):
            dest = lax.rem(c + d, C)

            @pl.when(dest != 0)
            def _():
                z_copy(j, dest, c).start()

    def panel_forward(j):
        @pl.when(c != 0)
        def _():
            p_copy(j, panel_ref.at[:, rows(j), :], 1).wait_recv()

            @pl.when(even)
            def _():
                p_copy(j, panel_ref.at[:, rows(j), :], 1).start()

                @pl.when(c + 2 < C)
                def _():
                    p_copy(j, panel_ref.at[:, rows(j), :], 2).start()

    def exchange(j):
        own_copy(j).wait()

        @pl.loop(1, C)
        def _(d):
            source = lax.rem(c + d, C)
            z_copy(j, source, source).wait_recv()

        for o in range(1, R):
            dest = lax.rem(r + o, R)

            @pl.loop(0, cap)
            def _(s):
                xout[j][o - 1, s] = zin[j][order_ref[dest * cap + s]]

            x_copy(j, o, dest, r).start()

        @pl.loop(0, cap)
        def _(s):
            xin[j][r * cap + s] = zin[j][order_ref[r * cap + s]]

    def assemble(j):
        front_copy(j).wait()
        for o in range(1, R):
            source = lax.rem(r + o, R)
            x_copy(j, o, source, source).wait_recv()

        @pl.loop(0, pb)
        def _(p):
            buf[j][p] = buf[j][p] + xin[j][place_ref[p]] + xin[j][place_ref[pb + p]]

        out_copy(j).start()

        @pl.when(c == 0)
        def _():
            panel_keep(j).start()
            p_copy(j, buf[j], 1).start()
            if C > 2:
                p_copy(j, buf[j], 2).start()

    for j in range(NCH + 1):
        if j < NCH:
            panel_forward(j)
            exchange(j)
        if j > 0:
            assemble(j - 1)

    @pl.when(c == 0)
    def _():
        for j in range(NCH):
            panel_keep(j).wait()

    owner = (c * PB) // pb
    start = lax.rem(c * PB, pb)

    def spread(index, first, out):
        def piece(k, dest):
            return pltpu.make_async_remote_copy(
                src_ref=panel_ref.at[pl.ds(first, PB)],
                dst_ref=out,
                send_sem=ms.at[index, k],
                recv_sem=mr.at[index],
                device_id={"row": dest},
                device_id_type=MESH,
            )

        return piece, pltpu.make_async_copy(panel_ref.at[pl.ds(first, PB)], out, ml.at[index])

    for index, holder, first, out in ((0, owner, start, match_ref), (1, 0, 0, diag_ref)):
        piece, local = spread(index, first, out)

        @pl.when(r == holder)
        def _():
            for o in range(1, R):
                piece(o - 1, lax.rem(r + o, R)).start()
            local.start()

        @pl.when(r != holder)
        def _():
            piece(0, lax.rem(r + 1, R)).wait_recv()

    for index, holder, first, out in ((0, owner, start, match_ref), (1, 0, 0, diag_ref)):
        piece, local = spread(index, first, out)

        @pl.when(r == holder)
        def _():
            for o in range(1, R):
                piece(o - 1, lax.rem(r + o, R)).wait_send()
            local.wait()

    for j in range(NCH):
        out_copy(j).wait()
        for o in range(1, R):
            x_copy(j, o, lax.rem(r + o, R), r).wait_send()

        @pl.loop(1, C)
        def _(d):
            z_copy(j, lax.rem(c + d, C), c).wait_send()

        @pl.when(even)
        def _():
            p_copy(j, panel_ref.at[:, rows(j), :], 1).wait_send()

            @pl.when(c + 2 < C)
            def _():
                p_copy(j, panel_ref.at[:, rows(j), :], 2).wait_send()


def move(order, place, send, front, C, R, nb, cap, pb, cols):
    f32 = jnp.float32
    hbm = pl.BlockSpec(memory_space=pl.ANY)
    smem = pl.BlockSpec(memory_space=pltpu.SMEM)
    dma = pltpu.SemaphoreType.DMA
    big = jax.ShapeDtypeStruct((pb, BLK, cols), f32)
    small = jax.ShapeDtypeStruct((PB, BLK, cols), f32)
    return pl.pallas_call(
        functools.partial(move_kernel, (C, R, nb, cap, pb)),
        out_shape=(big, big, small, small),
        in_specs=[smem, smem, hbm, hbm],
        out_specs=(hbm,) * 4,
        scratch_shapes=[pltpu.VMEM((C * nb, SUB, cols), f32)] * NCH
        + [pltpu.VMEM((R - 1, cap, SUB, cols), f32)] * NCH
        + [pltpu.VMEM((R * cap + 1, SUB, cols), f32)] * NCH
        + [pltpu.VMEM((pb, SUB, cols), f32)] * NCH
        + [
            dma((NCH, C)),
            dma((NCH, C)),
            dma((NCH,)),
            dma((NCH, R - 1)),
            dma((NCH, R)),
            dma((NCH,)),
            dma((NCH,)),
            dma((NCH, 2)),
            dma((NCH,)),
            dma((NCH,)),
            dma((2, R - 1)),
            dma((2,)),
            dma((2,)),
        ],
        compiler_params=pltpu.CompilerParams(
            collective_id=0, has_side_effects=True, vmem_limit_bytes=VMEM_LIMIT
        ),
        cost_estimate=pl.CostEstimate(flops=0, bytes_accessed=64 * 1024 * 1024, transcendentals=0),
    )(order, place, send, front)


STEP = 32


def dot(a, b, ca, cb):
    return lax.dot_general(
        a, b, (((ca,), (cb,)), ((), ())), precision=HI, preferred_element_type=jnp.float32
    )


def factor_kernel(diag_ref, match_ref, factor_ref, gain_ref, work):
    n = PANEL
    block = diag_ref[...]
    row = lax.broadcasted_iota(jnp.int32, (n, n), 0)
    lane = lax.broadcasted_iota(jnp.int32, (n, n), 1)
    work[:, :n] = 0.5 * (block + block.T)
    work[:, n:] = (row == lane).astype(jnp.float32)
    small_row = lax.broadcasted_iota(jnp.int32, (STEP, BLK), 0)
    small_lane = lax.broadcasted_iota(jnp.int32, (STEP, BLK), 1)
    unit = (small_lane == small_row + STEP).astype(jnp.float32)
    for k in range(0, n, STEP):
        tile = work[k:k + STEP, k // BLK * BLK:k // BLK * BLK + BLK]
        tile = pltpu.roll(tile, (BLK - k % BLK) % BLK, 1) if k % BLK else tile
        tile = jnp.where(small_lane < STEP, tile, unit)
        for i in range(STEP):
            scale = lax.rsqrt(tile[i:i + 1, i:i + 1])
            line = tile[i:i + 1, :] * scale
            column = jnp.where(small_row[:, :1] > i, tile[:, i:i + 1] * scale, 0.0)
            tile = jnp.where(small_row == i, line, tile - column * line)
        small_inverse = tile[:, STEP:2 * STEP]
        solved_rows = dot(small_inverse, work[k:k + STEP, :], 1, 0)
        work[k:k + STEP, :] = solved_rows
        if k + STEP < n:
            left = solved_rows[:, :n]
            update = dot(left, solved_rows, 0, 0)
            work[k + STEP:, :] = work[k + STEP:, :] - update[k + STEP:, :]
    upper = jnp.where(lane >= row, work[:, :n], 0.0)
    inverse = jnp.where(lane <= row, work[:, n:], 0.0)
    factor_ref[...] = upper.T
    solved = dot(inverse, match_ref[...], 1, 1)
    both = dot(inverse, solved, 0, 0)
    gain_ref[...] = jnp.where(lax.axis_index("col") == 0, -inverse.T, both)


def factorize(diag, match):
    shape = jax.ShapeDtypeStruct((PANEL, PANEL), jnp.float32)
    return pl.pallas_call(
        factor_kernel,
        out_shape=(shape, shape),
        in_specs=[pl.BlockSpec(memory_space=pltpu.VMEM)] * 2,
        out_specs=(pl.BlockSpec(memory_space=pltpu.VMEM),) * 2,
        scratch_shapes=[pltpu.VMEM((PANEL, 2 * PANEL), jnp.float32)],
        compiler_params=pltpu.CompilerParams(vmem_limit_bytes=32 * 1024 * 1024),
    )(diag, match)


def update_kernel(asm_ref, panel_ref, gain_ref, factor_ref, out_ref):
    first = lax.axis_index("col") == 0
    kept = jnp.where(first, 0.0, asm_ref[...])
    out_ref[...] = kept - dot(panel_ref[...], gain_ref[...], 1, 0)

    @pl.when((lax.axis_index("row") == 0) & (pl.program_id(0) == 0))
    def _():
        out_ref[:PANEL, :] = jnp.where(first, factor_ref[...], asm_ref[:PANEL, :])


def update(asm, panel, gain, factor, tile):
    rows, cols = asm.shape
    line = pl.BlockSpec((tile, cols), lambda i: (i, 0))
    whole = pl.BlockSpec((PANEL, cols), lambda i: (0, 0))
    return pl.pallas_call(
        update_kernel,
        grid=(rows // tile,),
        out_shape=jax.ShapeDtypeStruct((rows, cols), jnp.float32),
        in_specs=[line, line, whole, whole],
        out_specs=line,
        compiler_params=pltpu.CompilerParams(vmem_limit_bytes=32 * 1024 * 1024),
    )(asm, panel, gain, factor)


def body(front_window, children, row_map, col_map):
    R = lax.axis_size("row")
    C = lax.axis_size("col")
    r = lax.axis_index("row")
    rows_here, cols_here = front_window.shape
    child_rows, width = children.shape
    nb = child_rows // BLK
    qb = C * nb
    cap = qb // R
    pb = rows_here // BLK
    i32 = jnp.int32
    sibling = r // (R // 2)
    chosen = lax.dynamic_index_in_dim(col_map, sibling, 0, keepdims=False)
    wb = width // BLK
    ids = jnp.arange(wb, dtype=i32)
    inverse_cols = jnp.sum(jnp.where(chosen[None, :] == ids[:, None], ids[None, :], 0), axis=1)
    maps = row_map.reshape(R, qb)
    owners = maps // pb
    index = jnp.arange(qb, dtype=i32)
    earlier = index[None, :] < index[:, None]
    same = owners[:, :, None] == owners[:, None, :]
    rank = jnp.sum((same & earlier[None]).astype(i32), axis=2)
    mine = lax.dynamic_index_in_dim(owners * cap + rank, r, 0, keepdims=False)
    slots = jnp.arange(R * cap, dtype=i32)
    order = jnp.sum(jnp.where(mine[None, :] == slots[:, None], index[None, :], 0), axis=1)
    slot = (jnp.arange(R, dtype=i32)[:, None] * cap + rank).reshape(row_map.shape)
    wanted = r * pb + jnp.arange(pb, dtype=i32)
    hit = row_map[:, None, :] == wanted[None, :, None]
    found = jnp.sum(jnp.where(hit, slot[:, None, :] + 1, 0), axis=2)
    place = jnp.where(found > 0, found - 1, R * cap).reshape(-1)

    send = pack(children, inverse_cols, C, cols_here).reshape(C, nb, BLK, cols_here)
    asm, panel, match, diag = move(
        order, place, send, front_window.reshape(pb, BLK, cols_here), C, R, nb, cap, pb, cols_here
    )
    factor, gain = factorize(diag.reshape(PANEL, PANEL), match.reshape(PANEL, PANEL))
    return update(
        asm.reshape(rows_here, cols_here), panel.reshape(rows_here, cols_here), gain, factor, 1024
    )


def solution(mesh):
    placed = (
        P(("leaf", "row"), "col"),
        P(("leaf", "row", "col"), None),
        P("leaf", None),
        P("leaf", None),
    )
    return jax.shard_map(
        body, mesh=mesh, in_specs=placed, out_specs=P(("leaf", "row"), "col"), check_vma=False
    )
```

time: 1220 us -> 681 us (0.56)
  waiting for transfers between devices: 823 us -> 0 us
  Pallas kernels: 0 us -> 663 us
  local copies, waits for them, and re-layouts: 197 us -> 13.5 us
  other arithmetic: 103 us -> 3.27 us
  matrix products: 52.7 us -> 0 us
  starting transfers between devices: 16.3 us -> 0 us
  between operations: 15 us -> 0.08 us
    pallas_call x0 -> x4, Pallas kernels: none -> 663 us  [the longest x1 604 us: move(): pl.pallas_call(functools.partial(move_kernel, (C, R, nb, cap, pb)), out_s...]
    all_to_all x2 -> x0, waiting for transfers between devices: 521 us -> none  [the longest x1 354 us: body(): lax.all_to_all(spread, 'col', split_axis=1, concat_axis=0, tiled=True)]
    psum x3 -> x0, waiting for transfers between devices: 302 us -> none  [broadcast(): return lax.psum(kept, axis)]
    reshape x4 -> x0, local copies, waits for them, and re-layouts: 62 us -> none  [the longest x2 26.2 us: body(): assembled = front_window + added.reshape(rows_here, cols_here)]
    another operation x9 -> x0, other arithmetic: 53.7 us -> none  [the longest x6 34 us: body(): factor = jnp.linalg.cholesky(diagonal_block)]
    dot_general x3 -> x0, matrix products: 51.3 us -> none  [the longest x1 23 us: body(): update = jnp.dot(lower_panel, matching.T, precision=lax.Precision.HIGHEST)]
    gather x6 -> x0, local copies, waits for them, and re-layouts: 48.7 us -> none  [the longest x2 31.4 us: body(): jnp.take(children.reshape(child_rows, window_blocks, BLK), inverse_cols,...]
    select_n x10 -> x2, other arithmetic: 47 us -> 0.7 us  [the longest x1 0.69 us: body(): owners = maps // pb]
  transfers between devices with their start and end apart: 5 -> 0, of which waited for: 5 -> 0; matrix products, arithmetic and copies ran while one was open for 1% -> 0% of each run, Pallas kernels for 0% -> 0%
where the time goes in v1:
time: 681 us; the launch traced here: 680 us
  Pallas kernels  663 us (97%)
  local copies, waits for them, and re-layouts  13.5 us (2%)
    pallas_call x1, Pallas kernels, move(): pl.pallas_call(functools.partial(move_kernel, (C, R, nb, cap, pb)), out_s...  604 us
    pallas_call x1, Pallas kernels, factorize(): pl.pallas_call(factor_kernel, out_shape=(shape, shape), in_specs=[pl.Bloc...  28.7 us
    pallas_call x1, Pallas kernels, update(): pl.pallas_call(update_kernel, grid=(rows // tile,), out_shape=jax.ShapeDt...  17.6 us

profile of v1, /device:TPU:25, one launch (start us, length us, event | category | flops | bytes accessed | tf_op | source)
XLA Modules:
  0.0 680.3 jit_solution(5373625630045842327)
XLA Ops:
  0.0 0.0 copy-start
  0.0 0.7 copy-done
  0.7 0.1 select_reduce_fusion.2.index_ref
  0.8 0.7 and_select_fusion
  1.5 0.2 convert_reduce_fusion
  1.7 0.8 add_add_fusion
  2.5 0.8 select_reduce_fusion
  3.3 0.7 select_n.39.place_ref
  4.0 0.7 select_reduce_fusion.1.order_ref
  4.6 12.7 %shard_map.46 = f32[8,2048,256]{2,1,0:T(8,128)S(1)} custom-call(s32[16]{0:T(128)S(1)} %select_reduce_fusion.2.index_ref, f32[2048,2048]{1,0:T(8,128)} %child_ref.1), custom_call_target="tpu_custom_call" | custom-call | tf_op jit(solution)/shard_map/pallas_call | solution.py:27
  17.3 0.0 copy-start.2
  17.3 5.7 copy-done.2
  23.0 604.5 %shard_map.47 = (f32[96,128,256]{2,1,0:T(8,128)}, f32[96,128,256]{2,1,0:T(8,128)}, f32[2,128,256]{2,1,0:T(8,128)}, f32[2,128,256]{2,1,0:T(8,128)}) custom-call(s32[128]{0:T(128)} %select_reduce_fusion.1.order_ref, s32[192]{0:T(256)} %select_n.39.place_ref, f32[8,16,128,256]{3,2,1,0:T(8,128)} %bitcast.10, f32[96,128,256]{2,1,0:T(8,128)} %bitcast.14), custom_call_target="tpu_custom_call" | custom-call | bytes 67108864 | tf_op jit(solution)/shard_map/pallas_call | solution.py:250
  627.5 0.0 copy-start.4
  627.5 0.9 copy-done.4
  628.4 0.0 copy-start.5
  628.4 0.9 copy-done.5
  629.4 28.7 %shard_map.48 = (f32[256,256]{1,0:T(8,128)S(1)}, f32[256,256]{1,0:T(8,128)S(1)}) custom-call(f32[256,256]{1,0:T(8,128)S(1)} %bitcast.13, f32[256,256]{1,0:T(8,128)S(1)} %bitcast.12), custom_call_target="tpu_custom_call" | custom-call | tf_op jit(solution)/shard_map/pallas_call | solution.py:326
  658.1 0.0 copy-start.1
  658.1 0.0 copy-start.3
  658.1 4.6 copy-done.3
  662.7 17.6 %shard_map.49 = f32[12288,256]{1,0:T(8,128)} custom-call(f32[12288,256]{1,0:T(8,128)S(1)} %bitcast.11, f32[12288,256]{1,0:T(8,128)} %bitcast.15, f32[256,256]{1,0:T(8,128)S(1)} %get-tuple-element.15.gain_ref, f32[256,256]{1,0:T(8,128)S(1)} %get-tuple-element.16.factor_ref), custom_call_target="tpu_custom_call" | custom-call | tf_op jit(solution)/shard_map/pallas_call | solution.py:350
  680.3 0.0 copy-done.1
  (6 shorter events, 0.0 us)
Async XLA Ops:
  0.0 0.7 copy-start
  17.3 5.7 copy-start.2
  627.5 1.0 copy-start.4
  628.4 0.9 copy-start.5
  658.1 22.2 %copy-start.1 = (s32[2,16]{1,0:T(2,128)S(1)}, s32[2,16]{1,0:T(2,128)}, u32[]{:S(2)}) copy-start(s32[2,16]{1,0:T(2,128)} %param.7) | copy-start | bytes 388
  658.1 4.6 copy-start.3

commit v2 on v1

--- a/solution.py
+++ b/solution.py
@@ -104,33 +104,45 @@
         pl.semaphore_signal(barrier, inc=1, device_id={"row": lax.rem(r + o, R)}, device_id_type=MESH)
     pl.semaphore_wait(barrier, C + R - 2)
 
-    @pl.when(c != 0)
-    def _():
-        for j in range(NCH):
-            z_copy(j, 0, c).start()
-
-    for j in range(NCH):
-
+    def z_send(j, chosen):
         @pl.loop(1, C)
         def _(d):
             dest = lax.rem(c + d, C)
 
-            @pl.when(dest != 0)
+            @pl.when((dest != 0) & chosen(dest // 2))
             def _():
                 z_copy(j, dest, c).start()
 
+    def above(other):
+        return other > c // 2
+
+    def upward(other):
+        return other >= c // 2
+
+    def downward(other):
+        return other < c // 2
+
+    def not_above(other):
+        return other <= c // 2
+
+    @pl.when(jnp.logical_not(even))
+    def _():
+        for j in range(NCH):
+            z_copy(j, 0, c).start()
+            z_send(j, upward)
+        for j in range(NCH):
+            z_send(j, downward)
+
+    def panel_wait(j):
+        p_copy(j, panel_ref.at[:, rows(j), :], 1).wait_recv()
+
     def panel_forward(j):
-        @pl.when(c != 0)
-        def _():
-            p_copy(j, panel_ref.at[:, rows(j), :], 1).wait_recv()
-
-            @pl.when(even)
-            def _():
-                p_copy(j, panel_ref.at[:, rows(j), :], 1).start()
-
-                @pl.when(c + 2 < C)
-                def _():
-                    p_copy(j, panel_ref.at[:, rows(j), :], 2).start()
+        panel_wait(j)
+        p_copy(j, panel_ref.at[:, rows(j), :], 1).start()
+
+        @pl.when(c + 2 < C)
+        def _():
+            p_copy(j, panel_ref.at[:, rows(j), :], 2).start()
 
     def exchange(j):
         own_copy(j).wait()
@@ -172,9 +184,18 @@
             if C > 2:
                 p_copy(j, buf[j], 2).start()
 
+    @pl.when(even & (c != 0))
+    def _():
+        for j in range(NCH):
+            z_copy(j, 0, c).start()
+        for j in range(NCH):
+            panel_forward(j)
+            z_send(j, not_above)
+        for j in range(NCH):
+            z_send(j, above)
+
     for j in range(NCH + 1):
         if j < NCH:
-            panel_forward(j)
             exchange(j)
         if j > 0:
             assemble(j - 1)
@@ -182,7 +203,14 @@
     @pl.when(c == 0)
     def _():
         for j in range(NCH):
+            z_send(j, upward)
+        for j in range(NCH):
             panel_keep(j).wait()
+
+    @pl.when(jnp.logical_not(even))
+    def _():
+        for j in range(NCH):
+            panel_wait(j)
 
     owner = (c * PB) // pb
     start = lax.rem(c * PB, pb)

time: 681 us -> 718 us (1.054)
  Pallas kernels: 663 us -> 700 us
    pallas_call x1, Pallas kernels: 604 us -> 641 us  [move(): pl.pallas_call(functools.partial(move_kernel, (C, R, nb, cap, pb)), out_s...]
where the time goes in v2:
time: 718 us; the launch traced here: 717 us
  Pallas kernels  700 us (97%)
  local copies, waits for them, and re-layouts  13.5 us (2%)
    pallas_call x1, Pallas kernels, move(): pl.pallas_call(functools.partial(move_kernel, (C, R, nb, cap, pb)), out_s...  641 us
    pallas_call x1, Pallas kernels, factorize(): pl.pallas_call(factor_kernel, out_shape=(shape, shape), in_specs=[pl.Bloc...  28.7 us
    pallas_call x1, Pallas kernels, update(): pl.pallas_call(update_kernel, grid=(rows // tile,), out_shape=jax.ShapeDt...  17.6 us

profile of v2, /device:TPU:25, one launch (start us, length us, event | category | flops | bytes accessed | tf_op | source)
XLA Modules:
  0.0 716.8 jit_solution(8749761984108004853)
XLA Ops:
  0.0 0.0 copy-start
  0.0 0.7 copy-done
  0.7 0.1 select_reduce_fusion.2.index_ref
  0.8 0.7 and_select_fusion
  1.5 0.2 convert_reduce_fusion
  1.7 0.8 add_add_fusion
  2.5 0.8 select_reduce_fusion
  3.3 0.7 select_n.39.place_ref
  4.0 0.7 select_reduce_fusion.1.order_ref
  4.6 12.7 %shard_map.46 = f32[8,2048,256]{2,1,0:T(8,128)S(1)} custom-call(s32[16]{0:T(128)S(1)} %select_reduce_fusion.2.index_ref, f32[2048,2048]{1,0:T(8,128)} %child_ref.1), custom_call_target="tpu_custom_call" | custom-call | tf_op jit(solution)/shard_map/pallas_call | solution.py:27
  17.3 0.0 copy-start.2
  17.3 5.7 copy-done.2
  23.0 640.9 %shard_map.47 = (f32[96,128,256]{2,1,0:T(8,128)}, f32[96,128,256]{2,1,0:T(8,128)}, f32[2,128,256]{2,1,0:T(8,128)}, f32[2,128,256]{2,1,0:T(8,128)}) custom-call(s32[128]{0:T(128)} %select_reduce_fusion.1.order_ref, s32[192]{0:T(256)} %select_n.39.place_ref, f32[8,16,128,256]{3,2,1,0:T(8,128)} %bitcast.10, f32[96,128,256]{2,1,0:T(8,128)} %bitcast.14), custom_call_target="tpu_custom_call" | custom-call | bytes 67108864 | tf_op jit(solution)/shard_map/pallas_call | solution.py:278
  664.0 0.0 copy-start.4
  664.0 0.9 copy-done.4
  664.9 0.0 copy-start.5
  664.9 0.9 copy-done.5
  665.9 28.7 %shard_map.48 = (f32[256,256]{1,0:T(8,128)S(1)}, f32[256,256]{1,0:T(8,128)S(1)}) custom-call(f32[256,256]{1,0:T(8,128)S(1)} %bitcast.13, f32[256,256]{1,0:T(8,128)S(1)} %bitcast.12), custom_call_target="tpu_custom_call" | custom-call | tf_op jit(solution)/shard_map/pallas_call | solution.py:354
  694.6 0.0 copy-start.1
  694.6 0.0 copy-start.3
  694.6 4.6 copy-done.3
  699.1 17.6 %shard_map.49 = f32[12288,256]{1,0:T(8,128)} custom-call(f32[12288,256]{1,0:T(8,128)S(1)} %bitcast.11, f32[12288,256]{1,0:T(8,128)} %bitcast.15, f32[256,256]{1,0:T(8,128)S(1)} %get-tuple-element.15.gain_ref, f32[256,256]{1,0:T(8,128)S(1)} %get-tuple-element.16.factor_ref), custom_call_target="tpu_custom_call" | custom-call | tf_op jit(solution)/shard_map/pallas_call | solution.py:378
  716.8 0.0 copy-done.1
  (6 shorter events, 0.0 us)
Async XLA Ops:
  0.0 0.7 copy-start
  17.3 5.7 copy-start.2
  664.0 1.0 copy-start.4
  664.9 0.9 copy-start.5
  694.6 22.2 %copy-start.1 = (s32[2,16]{1,0:T(2,128)S(1)}, s32[2,16]{1,0:T(2,128)}, u32[]{:S(2)}) copy-start(s32[2,16]{1,0:T(2,128)} %param.7) | copy-start | bytes 388
  694.6 4.6 copy-start.3

commit v3 on v1

--- a/solution.py
+++ b/solution.py
@@ -33,7 +33,7 @@
             out_specs=pl.BlockSpec((1, child_rows, BLK), lambda k, idx: (k // per, 0, k % per)),
         ),
         out_shape=jax.ShapeDtypeStruct((col_count, child_rows, cols_here), jnp.float32),
-        compiler_params=pltpu.CompilerParams(vmem_limit_bytes=32 * 1024 * 1024),
+        compiler_params=pltpu.CompilerParams(vmem_limit_bytes=VMEM_LIMIT),
     )(inverse_cols, children)
 
 
@@ -104,12 +104,12 @@
         pl.semaphore_signal(barrier, inc=1, device_id={"row": lax.rem(r + o, R)}, device_id_type=MESH)
     pl.semaphore_wait(barrier, C + R - 2)
 
-    @pl.when(c != 0)
-    def _():
-        for j in range(NCH):
-            z_copy(j, 0, c).start()
-
     for j in range(NCH):
+
+        @pl.when(c != 0)
+        def _():
+            for t in range(2 * j, min(2 * j + 2, NCH)):
+                z_copy(t, 0, c).start()
 
         @pl.loop(1, C)
         def _(d):
@@ -174,10 +174,12 @@
 
     for j in range(NCH + 1):
         if j < NCH:
-            panel_forward(j)
             exchange(j)
         if j > 0:
             assemble(j - 1)
+
+    for j in range(NCH):
+        panel_forward(j)
 
     @pl.when(c == 0)
     def _():
@@ -329,7 +331,7 @@
         in_specs=[pl.BlockSpec(memory_space=pltpu.VMEM)] * 2,
         out_specs=(pl.BlockSpec(memory_space=pltpu.VMEM),) * 2,
         scratch_shapes=[pltpu.VMEM((PANEL, 2 * PANEL), jnp.float32)],
-        compiler_params=pltpu.CompilerParams(vmem_limit_bytes=32 * 1024 * 1024),
+        compiler_params=pltpu.CompilerParams(vmem_limit_bytes=VMEM_LIMIT),
     )(diag, match)
 
 
@@ -353,7 +355,7 @@
         out_shape=jax.ShapeDtypeStruct((rows, cols), jnp.float32),
         in_specs=[line, line, whole, whole],
         out_specs=line,
-        compiler_params=pltpu.CompilerParams(vmem_limit_bytes=32 * 1024 * 1024),
+        compiler_params=pltpu.CompilerParams(vmem_limit_bytes=VMEM_LIMIT),
     )(asm, panel, gain, factor)
 
 

time: 681 us -> 658 us (0.966)
  local copies, waits for them, and re-layouts: 13.5 us -> 1.34 us
  Pallas kernels: 663 us -> 652 us
    pallas_call x1, Pallas kernels: 604 us -> 583 us  [move(): pl.pallas_call(functools.partial(move_kernel, (C, R, nb, cap, pb)), out_s...]
    unnamed x12 -> x4, local copies, waits for them, and re-layouts: 12.9 us -> 0.68 us
where the time goes in v3:
time: 658 us; the launch traced here: 657 us
  Pallas kernels  652 us (99%)
    pallas_call x1, Pallas kernels, move(): pl.pallas_call(functools.partial(move_kernel, (C, R, nb, cap, pb)), out_s...  583 us
    pallas_call x1, Pallas kernels, factorize(): pl.pallas_call(factor_kernel, out_shape=(shape, shape), in_specs=[pl.Bloc...  30.5 us
    pallas_call x1, Pallas kernels, update(): pl.pallas_call(update_kernel, grid=(rows // tile,), out_shape=jax.ShapeDt...  20.1 us
    pallas_call x1, Pallas kernels, pack(): pl.pallas_call(pack_kernel, grid_spec=pltpu.PrefetchScalarGridSpec(num_sc...  18.2 us

profile of v3, /device:TPU:25, one launch (start us, length us, event | category | flops | bytes accessed | tf_op | source)
XLA Modules:
  0.0 656.7 jit_solution(11207922903347536929)
XLA Ops:
  0.0 0.0 copy-start
  0.0 0.7 copy-done
  0.7 0.6 select_reduce_fusion.2.index_ref
  1.3 0.7 and_select_fusion
  2.0 0.2 convert_reduce_fusion
  2.2 0.8 add_add_fusion
  3.0 0.8 select_reduce_fusion
  3.8 0.7 select_n.39.place_ref
  4.5 0.7 select_reduce_fusion.1.order_ref
  5.1 18.2 %shard_map.46 = f32[8,2048,256]{2,1,0:T(8,128)} custom-call(s32[16]{0:T(128)} %select_reduce_fusion.2.index_ref, f32[2048,2048]{1,0:T(8,128)} %child_ref.1), custom_call_target="tpu_custom_call" | custom-call | tf_op jit(solution)/shard_map/pallas_call | solution.py:27
  23.3 582.8 %shard_map.47 = (f32[96,128,256]{2,1,0:T(8,128)}, f32[96,128,256]{2,1,0:T(8,128)}, f32[2,128,256]{2,1,0:T(8,128)}, f32[2,128,256]{2,1,0:T(8,128)}) custom-call(s32[128]{0:T(128)} %select_reduce_fusion.1.order_ref, s32[192]{0:T(256)} %select_n.39.place_ref, f32[8,16,128,256]{3,2,1,0:T(8,128)} %bitcast.10, f32[96,128,256]{2,1,0:T(8,128)} %bitcast.11), custom_call_target="tpu_custom_call" | custom-call | bytes 67108864 | tf_op jit(solution)/shard_map/pallas_call | solution.py:252
  606.1 30.5 %shard_map.48 = (f32[256,256]{1,0:T(8,128)}, f32[256,256]{1,0:T(8,128)}) custom-call(f32[256,256]{1,0:T(8,128)} %bitcast.15, f32[256,256]{1,0:T(8,128)} %bitcast.14), custom_call_target="tpu_custom_call" | custom-call | tf_op jit(solution)/shard_map/pallas_call | solution.py:328
  636.6 0.0 copy-start.1
  636.6 20.1 %shard_map.49 = f32[12288,256]{1,0:T(8,128)} custom-call(f32[12288,256]{1,0:T(8,128)} %bitcast.12, f32[12288,256]{1,0:T(8,128)} %bitcast.13, f32[256,256]{1,0:T(8,128)} %get-tuple-element.15.gain_ref, f32[256,256]{1,0:T(8,128)} %get-tuple-element.16.factor_ref), custom_call_target="tpu_custom_call" | custom-call | tf_op jit(solution)/shard_map/pallas_call | solution.py:352
  656.7 0.0 copy-done.1
  (6 shorter events, 0.0 us)
Async XLA Ops:
  0.0 0.7 copy-start
  636.6 20.1 %copy-start.1 = (s32[2,16]{1,0:T(2,128)S(1)}, s32[2,16]{1,0:T(2,128)}, u32[]{:S(2)}) copy-start(s32[2,16]{1,0:T(2,128)} %param.7) | copy-start | bytes 388

commit v4 on v3

--- a/solution.py
+++ b/solution.py
@@ -44,6 +44,7 @@
     c = lax.axis_index("col")
     r = lax.axis_index("row")
     even = lax.rem(c, 2) == 0
+    relays = even & (c != 0) & (c + 2 < C)
 
     def rows(j):
         return pl.ds(j * SUB, SUB)
@@ -177,9 +178,21 @@
             exchange(j)
         if j > 0:
             assemble(j - 1)
+        if NCH - 3 <= j < NCH:
+
+            @pl.when(relays)
+            def _():
+                for t in range(2 * (j - NCH + 3), 2 * (j - NCH + 3) + 2):
+                    panel_forward(t)
 
     for j in range(NCH):
-        panel_forward(j)
+        if j < 6:
+
+            @pl.when(jnp.logical_not(relays))
+            def _():
+                panel_forward(j)
+        else:
+            panel_forward(j)
 
     @pl.when(c == 0)
     def _():

time: 658 us -> 617 us (0.938)
  Pallas kernels: 652 us -> 611 us
    pallas_call x1, Pallas kernels: 583 us -> 542 us  [move(): pl.pallas_call(functools.partial(move_kernel, (C, R, nb, cap, pb)), out_s...]
where the time goes in v4:
time: 617 us; the launch traced here: 616 us
  Pallas kernels  611 us (99%)
    pallas_call x1, Pallas kernels, move(): pl.pallas_call(functools.partial(move_kernel, (C, R, nb, cap, pb)), out_s...  542 us
    pallas_call x1, Pallas kernels, factorize(): pl.pallas_call(factor_kernel, out_shape=(shape, shape), in_specs=[pl.Bloc...  30.5 us
    pallas_call x1, Pallas kernels, update(): pl.pallas_call(update_kernel, grid=(rows // tile,), out_shape=jax.ShapeDt...  20.1 us
    pallas_call x1, Pallas kernels, pack(): pl.pallas_call(pack_kernel, grid_spec=pltpu.PrefetchScalarGridSpec(num_sc...  18.2 us

profile of v4, /device:TPU:25, one launch (start us, length us, event | category | flops | bytes accessed | tf_op | source)
XLA Modules:
  0.0 616.0 jit_solution(12767152504461319160)
XLA Ops:
  0.0 0.0 copy-start
  0.0 0.7 copy-done
  0.7 0.6 select_reduce_fusion.2.index_ref
  1.3 0.7 and_select_fusion
  2.0 0.2 convert_reduce_fusion
  2.2 0.8 add_add_fusion
  3.0 0.8 select_reduce_fusion
  3.8 0.7 select_n.39.place_ref
  4.5 0.7 select_reduce_fusion.1.order_ref
  5.1 18.2 %shard_map.46 = f32[8,2048,256]{2,1,0:T(8,128)} custom-call(s32[16]{0:T(128)} %select_reduce_fusion.2.index_ref, f32[2048,2048]{1,0:T(8,128)} %child_ref.1), custom_call_target="tpu_custom_call" | custom-call | tf_op jit(solution)/shard_map/pallas_call | solution.py:27
  23.3 542.0 %shard_map.47 = (f32[96,128,256]{2,1,0:T(8,128)}, f32[96,128,256]{2,1,0:T(8,128)}, f32[2,128,256]{2,1,0:T(8,128)}, f32[2,128,256]{2,1,0:T(8,128)}) custom-call(s32[128]{0:T(128)} %select_reduce_fusion.1.order_ref, s32[192]{0:T(256)} %select_n.39.place_ref, f32[8,16,128,256]{3,2,1,0:T(8,128)} %bitcast.10, f32[96,128,256]{2,1,0:T(8,128)} %bitcast.11), custom_call_target="tpu_custom_call" | custom-call | bytes 67108864 | tf_op jit(solution)/shard_map/pallas_call | solution.py:265
  565.4 30.5 %shard_map.48 = (f32[256,256]{1,0:T(8,128)}, f32[256,256]{1,0:T(8,128)}) custom-call(f32[256,256]{1,0:T(8,128)} %bitcast.15, f32[256,256]{1,0:T(8,128)} %bitcast.14), custom_call_target="tpu_custom_call" | custom-call | tf_op jit(solution)/shard_map/pallas_call | solution.py:341
  595.9 0.0 copy-start.1
  595.9 20.1 %shard_map.49 = f32[12288,256]{1,0:T(8,128)} custom-call(f32[12288,256]{1,0:T(8,128)} %bitcast.12, f32[12288,256]{1,0:T(8,128)} %bitcast.13, f32[256,256]{1,0:T(8,128)} %get-tuple-element.15.gain_ref, f32[256,256]{1,0:T(8,128)} %get-tuple-element.16.factor_ref), custom_call_target="tpu_custom_call" | custom-call | tf_op jit(solution)/shard_map/pallas_call | solution.py:365
  616.0 0.0 copy-done.1
  (6 shorter events, 0.0 us)
Async XLA Ops:
  0.0 0.7 copy-start
  595.9 20.1 %copy-start.1 = (s32[2,16]{1,0:T(2,128)S(1)}, s32[2,16]{1,0:T(2,128)}, u32[]{:S(2)}) copy-start(s32[2,16]{1,0:T(2,128)} %param.7) | copy-start | bytes 388
